TPU v7x, 512 devices: a whole 4x4x16 slice. The times are simulated.
512 devices in a mesh: ctx: 32 (over y, x, core), head: 16 (over z).
Axes of the slice: x: 4, y: 4, z: 16, core: 2. Of those that a mesh axis runs over, the one named last changes fastest.
Arguments:
- queries: bfloat16 [8192, 4096], P('ctx', 'head'), may hold values from -50 to 50
- keys: bfloat16 [8192, 4096], P('ctx', 'head'), may hold values from -9 to 9
- values: bfloat16 [8192, 4096], P('ctx', 'head'), may hold values from -9 to 9
- near_blocks: int32 [64, 4], P('ctx'), may hold values from 0 to 63, as said below
- near_count: int32 [64], P('ctx'), may hold values from 1 to 4
- head_scale: float32 [32], P('head'), may hold values from 0.2 to 4.2
- gain: float32 [4096], P('head'), may hold values from 0.5 to 1.5
- cotangent: bfloat16 [8192, 4096], P('ctx', 'head'), may hold values from -6 to 6
Outputs:
- mixed: bfloat16 [8192, 4096], P('ctx', 'head')
- grad_queries: bfloat16 [8192, 4096], P('ctx', 'head')
- grad_keys: bfloat16 [8192, 4096], P('ctx', 'head')
- grad_values: bfloat16 [8192, 4096], P('ctx', 'head')
Inputs may be any that keep to these rules, and one draw needn't show every extreme that they name: near_blocks[b, 0] = b; entries 1 to near_count[b] - 1 are distinct blocks other than b within 2 blocks of b; the later entries equal b.
All inputs are finite; a program needn't handle non-finite values.
Results may differ from a plain program's by a relative error of at most 0.022.
Values may be sent and summed in bfloat16 or wider, within the bound.
A program may use at most 64 MiB of HBM per device.

v0:
```python
import math
import jax
import jax.numpy as jnp
from jax import lax
from jax.sharding import PartitionSpec as P

HEADS = 32
HEAD_SIZE = 128
BLOCK_TOKENS = 128
NEAR_SLOTS = 4
RB = 2
LEV = 5
LOG_TWO = 0.6931471805599453
NEG_BIG = -1e30
NORM_EPS = 1e-05


def padded_2(cells, sides, width):
    for axis, dim in sides:
        count = lax.axis_size(axis)
        ends = count - 1
        head = lax.slice_in_dim(cells, 0, width, axis=dim)
        tail = lax.slice_in_dim(cells, cells.shape[dim] - width, cells.shape[dim], axis=dim)
        cells = jnp.concatenate(
            [
                lax.ppermute(tail, axis, [(i, (i + 1) % count) for i in range(ends)]),
                cells,
                lax.ppermute(head, axis, [((i + 1) % count, i) for i in range(ends)]),
            ],
            axis=dim,
        )
    return cells


def passed_along(value, axis, by):
    size = lax.axis_size(axis)
    pairs = [(i, i + by) for i in range(size) if 0 <= i + by < size]
    return lax.ppermute(value, axis, pairs)


def shortened(value):

    def short(part):
        return part.astype(jnp.bfloat16) if part.dtype == jnp.float32 else part

    return jax.tree.map(short, value)


def from_partner(value, axis, apart):
    mask = 2**apart
    pairs = [(source, source ^ mask) for source in range(lax.axis_size(axis))]
    return lax.ppermute(value, axis, pairs)


def body(queries, keys, values, near_blocks, near_count, head_scale, gain, cotangent):
    tok_rows = queries.shape[0]
    local_cols = queries.shape[1]
    heads_here = local_cols // HEAD_SIZE
    width = HEADS * HEAD_SIZE
    ctx_count = lax.axis_size("ctx")
    device = lax.axis_index("ctx")
    blocks_here = tok_rows // BLOCK_TOKENS
    margin = RB * BLOCK_TOKENS
    extended = blocks_here + 2 * RB
    columns = 2 * local_cols
    softmax_scale = 1.0 / math.sqrt(HEAD_SIZE)
    pair = jnp.concatenate([keys, values], axis=1)
    padded = padded_2(pair, (("ctx", 0),), margin)
    first_block = device * blocks_here - RB
    select = (near_blocks - first_block)[:, :, None] == jnp.arange(extended, dtype=jnp.int32)[
        None, None, :
    ]
    select_flat = select.reshape(blocks_here * NEAR_SLOTS, extended)
    near_pair = jnp.dot(
        select_flat.astype(jnp.bfloat16),
        padded.reshape(extended, BLOCK_TOKENS * columns),
        preferred_element_type=jnp.float32,
    )
    near_pair = near_pair.astype(jnp.bfloat16).reshape(
        blocks_here, NEAR_SLOTS, BLOCK_TOKENS, columns
    )
    valid = jnp.arange(NEAR_SLOTS, dtype=jnp.int32)[None, :] < near_count[:, None]
    key_mask = jnp.repeat(valid, BLOCK_TOKENS, axis=1)[:, None, :]
    factors = [2 ** (level_idx + 1) for level_idx in range(LEV)]
    groups = [min(2 ** (level_idx + 1), ctx_count) for level_idx in range(LEV)]
    pooled = [
        pair.astype(jnp.float32)
        .reshape(tok_rows // factors[level_idx], factors[level_idx], columns)
        .mean(axis=1)
        .astype(jnp.bfloat16)
        for level_idx in range(LEV)
    ]
    steps_count = max(groups).bit_length() - 1
    q_global = device * tok_rows + jnp.arange(tok_rows, dtype=jnp.int32)
    far_masks = []
    for level_idx in range(LEV):
        span_here = groups[level_idx] * tok_rows
        rows_level = span_here // factors[level_idx]
        group_first = device // groups[level_idx] * span_here
        key_first = group_first + jnp.arange(rows_level, dtype=jnp.int32) * factors[level_idx]
        keep = jnp.abs(key_first[None, :] // BLOCK_TOKENS - q_global[:, None] // BLOCK_TOKENS) > RB
        if level_idx > 0:
            prior = groups[level_idx - 1] * tok_rows
            keep = keep & (key_first[None, :] // prior != q_global[:, None] // prior)
        far_masks.append(keep)
    group_pair = list(pooled)
    shared = [level_idx for level_idx in range(LEV) if groups[level_idx] > 1]
    packed = jnp.concatenate([pooled[level_idx] for level_idx in shared], axis=0)
    everyone = lax.all_gather(packed, "ctx", axis=0, tiled=True).reshape(
        ctx_count, packed.shape[0], columns
    )
    offset = 0
    for level_idx in shared:
        count_rows = pooled[level_idx].shape[0]
        piece = everyone[:, offset : offset + count_rows]
        group_start = device // groups[level_idx] * groups[level_idx]
        chosen = lax.dynamic_slice_in_dim(piece, group_start, groups[level_idx], 0)
        group_pair[level_idx] = chosen.reshape(groups[level_idx] * count_rows, columns)
        offset = offset + count_rows
    saved = []
    attn_list = []
    for head_idx in range(heads_here):
        k_cols = slice(head_idx * HEAD_SIZE, (head_idx + 1) * HEAD_SIZE)
        v_cols = slice((heads_here + head_idx) * HEAD_SIZE, (heads_here + head_idx + 1) * HEAD_SIZE)
        q_head = queries[:, k_cols]
        query_blocks = q_head.reshape(blocks_here, BLOCK_TOKENS, HEAD_SIZE)
        near_key_rows = near_pair[:, :, :, k_cols].reshape(
            blocks_here, NEAR_SLOTS * BLOCK_TOKENS, HEAD_SIZE
        )
        near_value_rows = near_pair[:, :, :, v_cols].reshape(
            blocks_here, NEAR_SLOTS * BLOCK_TOKENS, HEAD_SIZE
        )
        near_score_rows = (
            jnp.einsum(
                "mne,mge->mng", query_blocks, near_key_rows, preferred_element_type=jnp.float32
            )
            * softmax_scale
        )
        near_score_rows = jnp.where(key_mask, near_score_rows, NEG_BIG)
        top = jnp.max(near_score_rows, axis=2).reshape(tok_rows)
        coarse_k = [group_pair[level_idx][:, k_cols] for level_idx in range(LEV)]
        coarse_v = [group_pair[level_idx][:, v_cols] for level_idx in range(LEV)]
        s_far = []
        for level_idx in range(LEV):
            scores = (
                jnp.einsum(
                    "td,kd->tk", q_head, coarse_k[level_idx], preferred_element_type=jnp.float32
                )
                * softmax_scale
                + (level_idx + 1) * LOG_TWO
            )
            scores = jnp.where(far_masks[level_idx], scores, NEG_BIG)
            s_far.append(scores)
            top = jnp.maximum(top, jnp.max(scores, axis=1))
        p_near = jnp.where(
            key_mask, jnp.exp(near_score_rows - top.reshape(blocks_here, BLOCK_TOKENS, 1)), 0.0
        )
        total = jnp.sum(p_near, axis=2).reshape(tok_rows)
        p_far = []
        for level_idx in range(LEV):
            exps = jnp.where(far_masks[level_idx], jnp.exp(s_far[level_idx] - top[:, None]), 0.0)
            p_far.append(exps)
            total = total + jnp.sum(exps, axis=1)
        prob_near = p_near / total.reshape(blocks_here, BLOCK_TOKENS, 1)
        near_weight_rows = prob_near.astype(jnp.bfloat16)
        attention_output = jnp.einsum(
            "itp,ipc->itc", near_weight_rows, near_value_rows, preferred_element_type=jnp.float32
        ).reshape(tok_rows, HEAD_SIZE)
        prob_far = []
        weight_far = []
        for level_idx in range(LEV):
            probs = p_far[level_idx] / total[:, None]
            weights_bf = probs.astype(jnp.bfloat16)
            prob_far.append(probs)
            weight_far.append(weights_bf)
            attention_output = attention_output + jnp.dot(
                weights_bf, coarse_v[level_idx], preferred_element_type=jnp.float32
            )
        attn_list.append(attention_output)
        saved.append(
            (
                q_head,
                query_blocks,
                near_key_rows,
                near_value_rows,
                prob_near,
                near_weight_rows,
                coarse_k,
                coarse_v,
                prob_far,
                weight_far,
            )
        )
    scaled = jnp.concatenate(
        [attn_list[head_idx] * head_scale[head_idx] for head_idx in range(heads_here)], axis=1
    )
    squares = lax.psum(jnp.sum(scaled * scaled, axis=1), "head")
    inv = lax.rsqrt(squares / width + NORM_EPS)
    mixed = (scaled * inv[:, None] * gain[None, :]).astype(jnp.bfloat16)
    back = cotangent.astype(jnp.float32) * gain[None, :]
    inner = lax.psum(jnp.sum(back * scaled, axis=1), "head")
    d_scaled = inv[:, None] * (back - scaled * (inv * inv * inner / width)[:, None])
    grad_q_list = []
    near_dk = []
    near_dv = []
    far_dk = [[] for level_idx in range(LEV)]
    far_dv = [[] for level_idx in range(LEV)]
    for head_idx in range(heads_here):
        (
            q_head,
            query_blocks,
            near_key_rows,
            near_value_rows,
            prob_near,
            near_weight_rows,
            coarse_k,
            coarse_v,
            prob_far,
            weight_far,
        ) = saved[head_idx]
        d_out = (
            d_scaled[:, head_idx * HEAD_SIZE : (head_idx + 1) * HEAD_SIZE] * head_scale[head_idx]
        ).astype(jnp.bfloat16)
        delta = jnp.sum(d_out.astype(jnp.float32) * attn_list[head_idx], axis=1)
        block_gradient = d_out.reshape(blocks_here, BLOCK_TOKENS, HEAD_SIZE)
        near_prob_gradient = jnp.einsum(
            "mne,mge->mng", block_gradient, near_value_rows, preferred_element_type=jnp.float32
        )
        near_score_gradient = (
            prob_near * (near_prob_gradient - delta.reshape(blocks_here, BLOCK_TOKENS, 1))
        ).astype(jnp.bfloat16)
        query_gradient = jnp.einsum(
            "itp,ipc->itc", near_score_gradient, near_key_rows, preferred_element_type=jnp.float32
        ).reshape(tok_rows, HEAD_SIZE)
        near_dk.append(
            jnp.einsum(
                "ail,aiz->alz",
                near_score_gradient,
                query_blocks,
                preferred_element_type=jnp.float32,
            )
            * softmax_scale
        )
        near_dv.append(
            jnp.einsum(
                "ail,aiz->alz", near_weight_rows, block_gradient, preferred_element_type=jnp.float32
            )
        )
        for level_idx in range(LEV):
            dp_far = jnp.einsum(
                "td,kd->tk", d_out, coarse_v[level_idx], preferred_element_type=jnp.float32
            )
            ds_far = (prob_far[level_idx] * (dp_far - delta[:, None])).astype(jnp.bfloat16)
            query_gradient = query_gradient + jnp.dot(
                ds_far, coarse_k[level_idx], preferred_element_type=jnp.float32
            )
            far_dk[level_idx].append(
                jnp.einsum("tk,td->kd", ds_far, q_head, preferred_element_type=jnp.float32)
                * softmax_scale
            )
            far_dv[level_idx].append(
                jnp.einsum(
                    "tk,td->kd", weight_far[level_idx], d_out, preferred_element_type=jnp.float32
                )
            )
        grad_q_list.append(query_gradient * softmax_scale)
    contrib = jnp.concatenate(near_dk + near_dv, axis=2).reshape(
        blocks_here * NEAR_SLOTS, BLOCK_TOKENS * columns
    )
    spread_ext = jnp.einsum(
        "xe,xc->ec", select_flat.astype(jnp.float32), contrib, precision=lax.Precision.HIGHEST
    )
    spread_ext = spread_ext.reshape(extended * BLOCK_TOKENS, columns)
    lower_rim = spread_ext[:margin]
    own_rows = spread_ext[margin : margin + tok_rows]
    upper_rim = spread_ext[margin + tok_rows :]
    from_above = passed_along(lower_rim.astype(jnp.bfloat16), "ctx", -1).astype(lower_rim.dtype)
    from_below = passed_along(upper_rim.astype(jnp.bfloat16), "ctx", 1).astype(upper_rim.dtype)
    grad_pair = own_rows + from_above + from_below
    far_grad = [
        jnp.concatenate(far_dk[level_idx] + far_dv[level_idx], axis=1) for level_idx in range(LEV)
    ]
    for bit_idx in reversed(range(steps_count)):
        active = [level_idx for level_idx in range(LEV) if groups[level_idx] > 2**bit_idx]
        upper_half = device // 2**bit_idx % 2 == 1
        sends = []
        keeps = []
        for level_idx in active:
            half_rows = far_grad[level_idx].shape[0] // 2
            lower_part = far_grad[level_idx][:half_rows]
            upper_part = far_grad[level_idx][half_rows:]
            keeps.append(jnp.where(upper_half, upper_part, lower_part))
            sends.append(jnp.where(upper_half, lower_part, upper_part))
        received = from_partner(shortened(jnp.concatenate(sends, axis=0)), "ctx", bit_idx)
        offset = 0
        for position, level_idx in enumerate(active):
            half_rows = keeps[position].shape[0]
            far_grad[level_idx] = keeps[position] + received[offset : offset + half_rows]
            offset = offset + half_rows
    for level_idx in range(LEV):
        factor = factors[level_idx]
        rows_level = far_grad[level_idx].shape[0]
        expanded = jnp.broadcast_to(
            (far_grad[level_idx] / factor)[:, None, :], (rows_level, factor, columns)
        )
        grad_pair = grad_pair + expanded.reshape(tok_rows, columns)
    grad_queries = jnp.concatenate(grad_q_list, axis=1).astype(jnp.bfloat16)
    grad_keys = grad_pair[:, :local_cols].astype(jnp.bfloat16)
    grad_values = grad_pair[:, local_cols:].astype(jnp.bfloat16)
    return (mixed, grad_queries, grad_keys, grad_values)


def solution(mesh):
    return jax.shard_map(
        body,
        mesh=mesh,
        in_specs=(
            P("ctx", "head"),
            P("ctx", "head"),
            P("ctx", "head"),
            P("ctx", None),
            P("ctx"),
            P("head"),
            P("head"),
            P("ctx", "head"),
        ),
        out_specs=(P("ctx", "head"), P("ctx", "head"), P("ctx", "head"), P("ctx", "head")),
        check_vma=False,
    )
```

profile of v0, /device:TPU:1, one launch (start us, length us, event | category | flops | bytes accessed | tf_op | source)
XLA Modules:
  0.0 259.7 jit_solution(10416025845603578630)
XLA Ops:
  7.2 1.0 concatenate.87
  8.3 1.0 concatenate.90
  9.3 1.0 concatenate.88
  10.3 1.0 concatenate.91
  13.6 4.5 %collective-permute-start = (bf16[256,512]{1,0:T(8,128)(2,1)S(1)}, bf16[256,512]{1,0:T(8,128)(2,1)S(1)}, u32[]{:S(2)}, u32[]{:S(2)}) collective-permute-start(bf16[256,512]{1,0:T(8,128)(2,1)S(1)} %constant_dynamic-update-slice_fusion), channel_id=1, source_target_pairs={{0,16},{16,32},{32,48},{48,64},{64,80},{80,96},{96,112},{112,128},... | collective-permute-start | bytes 786440 | tf_op jit(solution)/shard_map/ppermute | solution.py:26
  18.1 5.6 %collective-permute-start.1 = (bf16[256,512]{1,0:T(8,128)(2,1)S(1)}, bf16[256,512]{1,0:T(8,128)(2,1)S(1)}, u32[]{:S(2)}, u32[]{:S(2)}) collective-permute-start(bf16[256,512]{1,0:T(8,128)(2,1)S(1)} %constant_dynamic-update-slice_fusion), channel_id=1, source_target_pairs={{16,0},{32,16},{48,32},{64,48},{80,64},{96,80},{112,96},{128,112},... | collective-permute-start | bytes 786440 | tf_op jit(solution)/shard_map/ppermute | solution.py:28
  28.6 1.1 fusion.272
  30.2 56.8 %all-gather.2.cloned.1.call-done = bf16[7936,512]{1,0:T(8,128)(2,1)} async-done(((bf16[248,512]{1,0:T(8,128)(2,1)}), bf16[7936,512]{1,0:T(8,128)(2,1)}) %all-gather.2.cloned.1.call-update) | async-done | bytes 8126480 | tf_op jit(solution)/shard_map/all_gather | solution.py:109
  87.0 2.6 %slice.349 = bf16[32,128,512]{2,1,0:T(8,128)(2,1)S(1)} slice(bf16[32,248,512]{2,1,0:T(8,128)(2,1)} %bitcast.285), slice={[0:32], [0:128], [0:512]} | slice | bytes 8388608 | tf_op jit(solution)/shard_map/slice | solution.py:115
  89.7 1.8 slice.351
  91.5 1.3 slice.353
  92.8 1.1 slice.355
  93.9 1.0 slice_bitcast_fusion
  98.2 0.9 fusion.78
  101.5 1.1 fusion.101
  102.6 1.7 copy.148
  104.3 1.3 convolution_add_fusion.19
  105.6 1.3 convolution_add_fusion.18
  107.0 1.0 convolution_add_fusion.17
  108.0 1.0 convolution_add_fusion.16
  109.0 1.1 fusion.97
  110.1 1.7 copy.267
  111.8 1.2 convolution_add_fusion.14
  113.1 1.3 convolution_add_fusion.13
  114.4 1.0 convolution_add_fusion.12
  115.9 1.5 broadcast_multiply_fusion.1
  117.5 1.6 broadcast_multiply_fusion
  119.8 25.6 %all-reduce = (f32[256]{0:T(256)}, f32[256]{0:T(256)}) all-reduce(f32[256]{0:T(256)} %get-tuple-element.21, f32[256]{0:T(256)} %get-tuple-element.20), channel_id=1, replica_groups=mesh['ctx'=32,'head'=16] {'head'}, use_global_device_ids=true, to_apply=%region_30.31 | all-reduce | flops 512 | bytes 4096 | tf_op jit(solution)/shard_map/psum | solution.py:197
  146.2 1.8 subtract_multiply_fusion
  147.9 2.2 multiply_reduce_fusion.3
  150.2 1.9 fusion.130
  152.1 1.7 fusion.127
  153.8 0.9 fusion.115
  154.8 0.9 fusion.112
  165.5 1.0 fusion.289
  166.9 0.9 fusion.290
  172.3 4.4 %collective-permute-start.4 = (bf16[128,512]{1,0:T(8,128)(2,1)}, bf16[128,512]{1,0:T(8,128)(2,1)}, u32[]{:S(2)}, u32[]{:S(2)}) collective-permute-start(bf16[128,512]{1,0:T(8,128)(2,1)} %select_convert_fusion), channel_id=1, source_target_pairs={{0,256},{16,272},{32,288},{48,304},{64,320},{80,336},{96,352},{112... | collective-permute-start | bytes 393224 | tf_op jit(solution)/shard_map/ppermute | solution.py:52
  180.2 1.7 reshape.810
  181.9 2.8 %fusion.288 = (bf16[6,65536]{1,0:T(8,128)(2,1)S(1)}, f32[6,65536]{1,0:T(8,128)S(1)}) fusion(f32[8,65536]{1,0:T(8,128)} %reshape.810, s32[8]{0:T(128)S(1)} %copy-done.132), kind=kOutput, calls=%fused_computation.486 | convolution fusion | flops 38142000 | bytes 4456480 | tf_op jit(solution)/shard_map/xe,xc->ec/dot_general | solution.py:270
  185.0 0.9 convert_element_type.240
  186.0 9.1 %collective-permute-start.2 = (bf16[256,512]{1,0:T(8,128)(2,1)}, bf16[256,512]{1,0:T(8,128)(2,1)}, u32[]{:S(2)}, u32[]{:S(2)}) collective-permute-start(bf16[256,512]{1,0:T(8,128)(2,1)} %convert_element_type.240), channel_id=1, source_target_pairs={{16,0},{32,16},{48,32},{64,48},{80,64},{96,80},{112,96},{128,112},... | collective-permute-start | bytes 786440 | tf_op jit(solution)/shard_map/ppermute | solution.py:38
  196.0 2.1 collective-permute-start.3
  198.1 1.1 convolution_add_fusion.9
  199.3 1.2 convolution_add_fusion.8
  200.5 1.1 convolution_add_fusion.7
  201.6 1.1 convolution_add_fusion.6
  202.8 1.2 convolution_add_fusion.4
  204.0 1.1 convolution_add_fusion.3
  205.1 1.8 convolution_add_fusion.2
  207.3 1.1 convert_add_fusion.3
  208.5 2.2 collective-permute-start.5
  210.7 4.8 %collective-permute-done.5 = bf16[192,512]{1,0:T(8,128)(2,1)S(1)} collective-permute-done((bf16[192,512]{1,0:T(8,128)(2,1)S(1)}, bf16[192,512]{1,0:T(8,128)(2,1)S(1)}, u32[]{:S(2)}, u32[]{:S(2)}) %collective-permute-start.5) | collective-permute-done | bytes 196640 | tf_op jit(solution)/shard_map/ppermute | solution.py:52
  215.7 5.5 %collective-permute-start.6 = (bf16[224,512]{1,0:T(8,128)(2,1)S(1)}, bf16[224,512]{1,0:T(8,128)(2,1)S(1)}, u32[]{:S(2)}, u32[]{:S(2)}) collective-permute-start(bf16[224,512]{1,0:T(8,128)(2,1)S(1)} %pad_maximum_fusion.9), channel_id=1, source_target_pairs={{0,64},{16,80},{32,96},{48,112},{64,0},{80,16},{96,32},{112,48},{1... | collective-permute-start | bytes 688136 | tf_op jit(solution)/shard_map/ppermute | solution.py:52
  221.9 3.7 %collective-permute-done.6 = bf16[224,512]{1,0:T(8,128)(2,1)S(1)} collective-permute-done((bf16[224,512]{1,0:T(8,128)(2,1)S(1)}, bf16[224,512]{1,0:T(8,128)(2,1)S(1)}, u32[]{:S(2)}, u32[]{:S(2)}) %collective-permute-start.6) | collective-permute-done | bytes 229408 | tf_op jit(solution)/shard_map/ppermute | solution.py:52
  226.5 4.9 %collective-permute-start.7 = (bf16[240,512]{1,0:T(8,128)(2,1)}, bf16[240,512]{1,0:T(8,128)(2,1)}, u32[]{:S(2)}, u32[]{:S(2)}) collective-permute-start(bf16[240,512]{1,0:T(8,128)(2,1)} %pad_maximum_fusion.8), channel_id=1, source_target_pairs={{0,32},{16,48},{32,0},{48,16},{64,96},{80,112},{96,64},{112,80},{1... | collective-permute-start | bytes 737288 | tf_op jit(solution)/shard_map/ppermute | solution.py:52
  231.5 1.7 fusion.61
  233.2 1.1 slice.379
  234.3 1.5 slice.299
  235.8 1.7 copy.210
  237.5 1.2 convolution_add_fusion.1
  238.7 1.0 convert_add_fusion
  244.7 3.4 %collective-permute-start.8 = (bf16[248,512]{1,0:T(8,128)(2,1)}, bf16[248,512]{1,0:T(8,128)(2,1)S(1)}, u32[]{:S(2)}, u32[]{:S(2)}) collective-permute-start(bf16[248,512]{1,0:T(8,128)(2,1)} %constant_dynamic-update-slice_fusion.4), channel_id=1, source_target_pairs={{0,16},{16,0},{32,48},{48,32},{64,80},{80,64},{96,112},{112,96},{1... | collective-permute-start | bytes 761864 | tf_op jit(solution)/shard_map/ppermute | solution.py:52
  248.1 1.1 fusion.60
  250.9 1.3 fusion.62
  (443 shorter events, 42.7 us)
Async XLA Ops:
  7.2 79.8 %all-gather.2.cloned.1.call-start = ((), (), s32[]{:S(2)}) async-start(), calls=%async_computation | async-start | bytes 8380416 | tf_op jit(solution)/shard_map/all_gather | solution.py:109
  8.3 17.3 %copy-start.130 = (f32[2]{0:T(128)S(1)}, f32[2]{0:T(128)}, u32[]{:S(2)}) copy-start(f32[2]{0:T(128)} %param.13) | copy-start | bytes 28
  8.3 17.9 %copy-start.146 = (s32[2]{0:T(128)S(1)}, s32[2]{0:T(128)}, u32[]{:S(2)}) copy-start(s32[2]{0:T(128)} %param.12) | copy-start | bytes 28
  8.3 18.1 %copy-start.145 = (s32[2,4]{1,0:T(2,128)S(1)}, s32[2,4]{1,0:T(2,128)}, u32[]{:S(2)}) copy-start(s32[2,4]{1,0:T(2,128)} %param.11) | copy-start | bytes 100
  9.2 17.3 %copy-start.71 = (bf16[256,256]{1,0:T(8,128)(2,1)S(1)}, bf16[256,256]{1,0:T(8,128)(2,1)}, u32[]{:S(2)}) copy-start(bf16[256,256]{1,0:T(8,128)(2,1)} %param.15) | copy-start | bytes 393220
  10.3 16.5 %copy-start = (bf16[256,256]{1,0:T(8,128)(2,1)S(1)}, bf16[256,256]{1,0:T(8,128)(2,1)}, u32[]{:S(2)}) copy-start(bf16[256,256]{1,0:T(8,128)(2,1)} %param.8) | copy-start | bytes 393220
  13.6 13.2 %collective-permute-start = (bf16[256,512]{1,0:T(8,128)(2,1)S(1)}, bf16[256,512]{1,0:T(8,128)(2,1)S(1)}, u32[]{:S(2)}, u32[]{:S(2)}) collective-permute-start(bf16[256,512]{1,0:T(8,128)(2,1)S(1)} %constant_dynamic-update-slice_fusion), channel_id=1, source_target_pairs={{0,16},{16,32},{32,48},{48,64},{64,80},{80,96},{96,112},{112,128},... | collective-permute-start | bytes 786440 | tf_op jit(solution)/shard_map/ppermute | solution.py:26
  18.1 8.7 %collective-permute-start.1 = (bf16[256,512]{1,0:T(8,128)(2,1)S(1)}, bf16[256,512]{1,0:T(8,128)(2,1)S(1)}, u32[]{:S(2)}, u32[]{:S(2)}) collective-permute-start(bf16[256,512]{1,0:T(8,128)(2,1)S(1)} %constant_dynamic-update-slice_fusion), channel_id=1, source_target_pairs={{16,0},{32,16},{48,32},{64,48},{80,64},{96,80},{112,96},{128,112},... | collective-permute-start | bytes 786440 | tf_op jit(solution)/shard_map/ppermute | solution.py:28
  23.7 73.8 %copy-start.81 = (s32[256]{0:T(256)}, s32[256]{0:T(256)S(1)}, u32[]{:S(2)}) copy-start(s32[256]{0:T(256)S(1)} %and_select_fusion.12) | copy-start | bytes 3076
  23.8 72.0 %copy-start.86 = (s32[256]{0:T(256)}, s32[256]{0:T(256)S(1)}, u32[]{:S(2)}) copy-start(s32[256]{0:T(256)S(1)} %get-tuple-element.101) | copy-start | bytes 3076
  23.8 72.6 %copy-start.98 = (s32[256]{0:T(256)}, s32[256]{0:T(256)S(1)}, u32[]{:S(2)}) copy-start(s32[256]{0:T(256)S(1)} %get-tuple-element.100) | copy-start | bytes 3076
  23.8 72.5 %copy-start.101 = (s32[256]{0:T(256)}, s32[256]{0:T(256)S(1)}, u32[]{:S(2)}) copy-start(s32[256]{0:T(256)S(1)} %get-tuple-element.98) | copy-start | bytes 3076
  23.8 72.5 %copy-start.104 = (s32[256]{0:T(256)}, s32[256]{0:T(256)S(1)}, u32[]{:S(2)}) copy-start(s32[256]{0:T(256)S(1)} %get-tuple-element.99) | copy-start | bytes 3076
  25.0 70.7 %copy-start.111 = (s32[256]{0:T(256)}, s32[256]{0:T(256)S(1)}, u32[]{:S(2)}) copy-start(s32[256]{0:T(256)S(1)} %get-tuple-element.102) | copy-start | bytes 3076
  25.0 70.7 %copy-start.114 = (s32[256]{0:T(256)}, s32[256]{0:T(256)S(1)}, u32[]{:S(2)}) copy-start(s32[256]{0:T(256)S(1)} %get-tuple-element.103) | copy-start | bytes 3076
  26.4 68.8 %copy-start.133 = (s32[256]{0:T(256)}, s32[256]{0:T(256)S(1)}, u32[]{:S(2)}) copy-start(s32[256]{0:T(256)S(1)} %and_select_fusion.13) | copy-start | bytes 3076
  94.9 63.1 %copy-start.10 = (bf16[256,512]{1,0:T(8,128)(2,1)}, bf16[256,512]{1,0:T(8,128)(2,1)S(1)}, u32[]{:S(2)}) copy-start(bf16[256,512]{1,0:T(8,128)(2,1)S(1)} %slice_bitcast_fusion) | copy-start | bytes 786436
  94.9 68.7 %copy-start.7 = (bf16[2,128,512]{2,1,0:T(8,128)(2,1)}, bf16[2,128,512]{2,1,0:T(8,128)(2,1)S(1)}, u32[]{:S(2)}) copy-start(bf16[2,128,512]{2,1,0:T(8,128)(2,1)S(1)} %constant_dynamic-slice_fusion.3) | copy-start | bytes 786436
  95.2 16.6 %copy-start.40 = (f32[256,256]{0,1:T(8,128)}, f32[256,256]{0,1:T(8,128)S(1)}, u32[]{:S(2)}) copy-start(f32[256,256]{0,1:T(8,128)S(1)} %get-tuple-element.83) | copy-start | bytes 786436
  95.4 65.3 %copy-start.8 = (bf16[4,64,512]{2,1,0:T(8,128)(2,1)}, bf16[4,64,512]{2,1,0:T(8,128)(2,1)S(1)}, u32[]{:S(2)}) copy-start(bf16[4,64,512]{2,1,0:T(8,128)(2,1)S(1)} %constant_dynamic-slice_fusion.2) | copy-start | bytes 786436
  96.1 60.1 %copy-start.9 = (bf16[8,32,512]{2,1,0:T(8,128)(2,1)}, bf16[8,32,512]{2,1,0:T(8,128)(2,1)S(1)}, u32[]{:S(2)}) copy-start(bf16[8,32,512]{2,1,0:T(8,128)(2,1)S(1)} %constant_dynamic-slice_fusion.1) | copy-start | bytes 786436
  96.7 104.9 %copy-start.6 = (bf16[16,16,512]{2,1,0:T(8,128)(2,1)}, bf16[16,16,512]{2,1,0:T(8,128)(2,1)S(1)}, u32[]{:S(2)}) copy-start(bf16[16,16,512]{2,1,0:T(8,128)(2,1)S(1)} %constant_dynamic-slice_fusion) | copy-start | bytes 786436
  117.5 28.7 %copy-start.28 = (f32[256,128]{0,1:T(8,128)}, f32[256,128]{0,1:T(8,128)S(1)}, u32[]{:S(2)}) copy-start(f32[256,128]{0,1:T(8,128)S(1)} %get-tuple-element.88) | copy-start | bytes 393220
  119.1 27.1 %copy-start.29 = (f32[256,128]{0,1:T(8,128)}, f32[256,128]{0,1:T(8,128)S(1)}, u32[]{:S(2)}) copy-start(f32[256,128]{0,1:T(8,128)S(1)} %get-tuple-element.86) | copy-start | bytes 393220
  146.1 7.7 %copy-start.50 = (f32[256,256]{0,1:T(8,128)S(1)}, f32[256,256]{0,1:T(8,128)}, u32[]{:S(2)}) copy-start(f32[256,256]{0,1:T(8,128)} %copy-done.48) | copy-start | bytes 786436
  146.1 7.7 %copy-start.85 = (s32[256]{0:T(256)S(1)}, s32[256]{0:T(256)}, u32[]{:S(2)}) copy-start(s32[256]{0:T(256)} %copy-done.81) | copy-start | bytes 3076
  146.1 7.7 %copy-start.100 = (s32[256]{0:T(256)S(1)}, s32[256]{0:T(256)}, u32[]{:S(2)}) copy-start(s32[256]{0:T(256)} %copy-done.98) | copy-start | bytes 3076
  146.2 7.7 %copy-start.103 = (s32[256]{0:T(256)S(1)}, s32[256]{0:T(256)}, u32[]{:S(2)}) copy-start(s32[256]{0:T(256)} %copy-done.101) | copy-start | bytes 3076
  155.9 11.9 %copy-start.22 = (bf16[256,256]{0,1:T(8,128)(2,1)}, bf16[256,256]{0,1:T(8,128)(2,1)S(1)}, u32[]{:S(2)}) copy-start(bf16[256,256]{0,1:T(8,128)(2,1)S(1)} %fusion.50) | copy-start | bytes 393220
  156.2 13.3 %copy-start.21 = (bf16[256,256]{0,1:T(8,128)(2,1)}, bf16[256,256]{0,1:T(8,128)(2,1)S(1)}, u32[]{:S(2)}) copy-start(bf16[256,256]{0,1:T(8,128)(2,1)S(1)} %fusion.51) | copy-start | bytes 393220
  156.4 12.2 %copy-start.19 = (bf16[256,256]{0,1:T(8,128)(2,1)}, bf16[256,256]{0,1:T(8,128)(2,1)S(1)}, u32[]{:S(2)}) copy-start(bf16[256,256]{0,1:T(8,128)(2,1)S(1)} %fusion.55) | copy-start | bytes 393220
  157.2 13.2 %copy-start.16 = (bf16[256,256]{0,1:T(8,128)(2,1)}, bf16[256,256]{0,1:T(8,128)(2,1)S(1)}, u32[]{:S(2)}) copy-start(bf16[256,256]{0,1:T(8,128)(2,1)S(1)} %fusion.56) | copy-start | bytes 393220
  158.0 13.2 %copy-start.17 = (bf16[256,256]{0,1:T(8,128)(2,1)}, bf16[256,256]{0,1:T(8,128)(2,1)S(1)}, u32[]{:S(2)}) copy-start(bf16[256,256]{0,1:T(8,128)(2,1)S(1)} %fusion.52) | copy-start | bytes 393220
  158.7 12.6 %copy-start.14 = (bf16[256,256]{0,1:T(8,128)(2,1)}, bf16[256,256]{0,1:T(8,128)(2,1)S(1)}, u32[]{:S(2)}) copy-start(bf16[256,256]{0,1:T(8,128)(2,1)S(1)} %fusion.57) | copy-start | bytes 393220
  160.8 15.9 %copy-start.25 = (bf16[256,256]{0,1:T(8,128)(2,1)}, bf16[256,256]{0,1:T(8,128)(2,1)S(1)}, u32[]{:S(2)}) copy-start(bf16[256,256]{0,1:T(8,128)(2,1)S(1)} %fusion.49) | copy-start | bytes 393220
  161.5 16.0 %copy-start.23 = (bf16[256,256]{0,1:T(8,128)(2,1)}, bf16[256,256]{0,1:T(8,128)(2,1)S(1)}, u32[]{:S(2)}) copy-start(bf16[256,256]{0,1:T(8,128)(2,1)S(1)} %fusion.54) | copy-start | bytes 393220
  163.6 14.8 %copy-start.27 = (bf16[256,256]{0,1:T(8,128)(2,1)}, bf16[256,256]{0,1:T(8,128)(2,1)S(1)}, u32[]{:S(2)}) copy-start(bf16[256,256]{0,1:T(8,128)(2,1)S(1)} %fusion.48) | copy-start | bytes 393220
  163.8 15.4 %copy-start.26 = (bf16[256,256]{0,1:T(8,128)(2,1)}, bf16[256,256]{0,1:T(8,128)(2,1)S(1)}, u32[]{:S(2)}) copy-start(bf16[256,256]{0,1:T(8,128)(2,1)S(1)} %fusion.53) | copy-start | bytes 393220
  172.3 35.1 %collective-permute-start.4 = (bf16[128,512]{1,0:T(8,128)(2,1)}, bf16[128,512]{1,0:T(8,128)(2,1)}, u32[]{:S(2)}, u32[]{:S(2)}) collective-permute-start(bf16[128,512]{1,0:T(8,128)(2,1)} %select_convert_fusion), channel_id=1, source_target_pairs={{0,256},{16,272},{32,288},{48,304},{64,320},{80,336},{96,352},{112... | collective-permute-start | bytes 393224 | tf_op jit(solution)/shard_map/ppermute | solution.py:52
  184.6 13.4 %copy-start.12 = (f32[2,128,128]{2,1,0:T(8,128)S(1)}, f32[2,128,128]{2,1,0:T(8,128)}, u32[]{:S(2)}) copy-start(f32[2,128,128]{2,1,0:T(8,128)} %fusion.289) | copy-start | bytes 393220
  186.0 16.8 %copy-start.13 = (f32[2,128,128]{2,1,0:T(8,128)S(1)}, f32[2,128,128]{2,1,0:T(8,128)}, u32[]{:S(2)}) copy-start(f32[2,128,128]{2,1,0:T(8,128)} %fusion.290) | copy-start | bytes 393220
  186.0 64.9 %collective-permute-start.2 = (bf16[256,512]{1,0:T(8,128)(2,1)}, bf16[256,512]{1,0:T(8,128)(2,1)}, u32[]{:S(2)}, u32[]{:S(2)}) collective-permute-start(bf16[256,512]{1,0:T(8,128)(2,1)} %convert_element_type.240), channel_id=1, source_target_pairs={{16,0},{32,16},{48,32},{64,48},{80,64},{96,80},{112,96},{128,112},... | collective-permute-start | bytes 786440 | tf_op jit(solution)/shard_map/ppermute | solution.py:38
  196.0 8.0 %copy-start.24 = (bf16[256,256]{0,1:T(8,128)(2,1)S(1)}, bf16[256,256]{0,1:T(8,128)(2,1)}, u32[]{:S(2)}) copy-start(bf16[256,256]{0,1:T(8,128)(2,1)} %copy-done.23) | copy-start | bytes 393220
  196.0 9.1 %copy-start.20 = (bf16[256,256]{0,1:T(8,128)(2,1)S(1)}, bf16[256,256]{0,1:T(8,128)(2,1)}, u32[]{:S(2)}) copy-start(bf16[256,256]{0,1:T(8,128)(2,1)} %copy-done.19) | copy-start | bytes 393220
  196.0 10.9 %copy-start.32 = (f32[256,128]{1,0:T(8,128)S(1)}, f32[256,128]{1,0:T(8,128)}, u32[]{:S(2)}) copy-start(f32[256,128]{1,0:T(8,128)} %convolution_multiply_fusion.19) | copy-start | bytes 393220
  196.0 10.9 %copy-start.33 = (f32[256,128]{1,0:T(8,128)S(1)}, f32[256,128]{1,0:T(8,128)}, u32[]{:S(2)}) copy-start(f32[256,128]{1,0:T(8,128)} %convolution_multiply_fusion.18) | copy-start | bytes 393220
  196.0 10.9 %copy-start.74 = (f32[256,128]{1,0:T(8,128)S(1)}, f32[256,128]{1,0:T(8,128)}, u32[]{:S(2)}) copy-start(f32[256,128]{1,0:T(8,128)} %fusion.130) | copy-start | bytes 393220
  196.0 10.9 %copy-start.75 = (f32[256,128]{1,0:T(8,128)S(1)}, f32[256,128]{1,0:T(8,128)}, u32[]{:S(2)}) copy-start(f32[256,128]{1,0:T(8,128)} %fusion.115) | copy-start | bytes 393220
  196.0 54.8 %collective-permute-start.3 = (bf16[256,512]{1,0:T(8,128)(2,1)}, bf16[256,512]{1,0:T(8,128)(2,1)}, u32[]{:S(2)}, u32[]{:S(2)}) collective-permute-start(bf16[256,512]{1,0:T(8,128)(2,1)} %convert_element_type.242), channel_id=1, source_target_pairs={{0,16},{16,32},{32,48},{48,64},{64,80},{80,96},{96,112},{112,128},... | collective-permute-start | bytes 786440 | tf_op jit(solution)/shard_map/ppermute | solution.py:38
  199.2 7.8 %copy-start.30 = (f32[256,128]{1,0:T(8,128)S(1)}, f32[256,128]{1,0:T(8,128)}, u32[]{:S(2)}) copy-start(f32[256,128]{1,0:T(8,128)} %convolution_multiply_fusion.17) | copy-start | bytes 393220
  199.2 7.8 %copy-start.31 = (f32[256,128]{1,0:T(8,128)S(1)}, f32[256,128]{1,0:T(8,128)}, u32[]{:S(2)}) copy-start(f32[256,128]{1,0:T(8,128)} %convolution_multiply_fusion.16) | copy-start | bytes 393220
  199.2 7.8 %copy-start.72 = (f32[256,128]{1,0:T(8,128)S(1)}, f32[256,128]{1,0:T(8,128)}, u32[]{:S(2)}) copy-start(f32[256,128]{1,0:T(8,128)} %fusion.127) | copy-start | bytes 393220
  199.3 7.8 %copy-start.73 = (f32[256,128]{1,0:T(8,128)S(1)}, f32[256,128]{1,0:T(8,128)}, u32[]{:S(2)}) copy-start(f32[256,128]{1,0:T(8,128)} %fusion.112) | copy-start | bytes 393220
  207.3 8.4 %copy-start.3 = (f32[256,512]{1,0:T(8,128)}, f32[256,512]{1,0:T(8,128)S(1)}, u32[]{:S(2)}) copy-start(f32[256,512]{1,0:T(8,128)S(1)} %pad_maximum_fusion.3) | copy-start | bytes 1572868
  208.5 7.1 %collective-permute-start.5 = (bf16[192,512]{1,0:T(8,128)(2,1)S(1)}, bf16[192,512]{1,0:T(8,128)(2,1)S(1)}, u32[]{:S(2)}, u32[]{:S(2)}) collective-permute-start(bf16[192,512]{1,0:T(8,128)(2,1)S(1)} %pad_maximum_fusion.10), channel_id=1, source_target_pairs={{0,128},{16,144},{32,160},{48,176},{64,192},{80,208},{96,224},{112... | collective-permute-start | bytes 589832 | tf_op jit(solution)/shard_map/ppermute | solution.py:52
  215.6 15.9 %copy-start.18 = (bf16[256,256]{0,1:T(8,128)(2,1)S(1)}, bf16[256,256]{0,1:T(8,128)(2,1)}, u32[]{:S(2)}) copy-start(bf16[256,256]{0,1:T(8,128)(2,1)} %copy-done.17) | copy-start | bytes 393220
  215.7 9.9 %collective-permute-start.6 = (bf16[224,512]{1,0:T(8,128)(2,1)S(1)}, bf16[224,512]{1,0:T(8,128)(2,1)S(1)}, u32[]{:S(2)}, u32[]{:S(2)}) collective-permute-start(bf16[224,512]{1,0:T(8,128)(2,1)S(1)} %pad_maximum_fusion.9), channel_id=1, source_target_pairs={{0,64},{16,80},{32,96},{48,112},{64,0},{80,16},{96,32},{112,48},{1... | collective-permute-start | bytes 688136 | tf_op jit(solution)/shard_map/ppermute | solution.py:52
  225.7 14.0 %copy-start.5 = (f32[64,512]{1,0:T(8,128)}, f32[64,512]{1,0:T(8,128)S(1)}, u32[]{:S(2)}) copy-start(f32[64,512]{1,0:T(8,128)S(1)} %convert_add_fusion.5) | copy-start | bytes 393220
  225.7 13.0 %copy-start.4 = (f32[256,512]{1,0:T(8,128)S(1)}, f32[256,512]{1,0:T(8,128)}, u32[]{:S(2)}) copy-start(f32[256,512]{1,0:T(8,128)} %copy-done.3) | copy-start | bytes 1572868
  226.5 12.2 %collective-permute-start.7 = (bf16[240,512]{1,0:T(8,128)(2,1)}, bf16[240,512]{1,0:T(8,128)(2,1)}, u32[]{:S(2)}, u32[]{:S(2)}) collective-permute-start(bf16[240,512]{1,0:T(8,128)(2,1)} %pad_maximum_fusion.8), channel_id=1, source_target_pairs={{0,32},{16,48},{32,0},{48,16},{64,96},{80,112},{96,64},{112,80},{1... | collective-permute-start | bytes 737288 | tf_op jit(solution)/shard_map/ppermute | solution.py:52
  234.3 9.1 %copy-start.39 = (f32[32,512]{1,0:T(8,128)S(1)}, f32[32,512]{1,0:T(8,128)}, u32[]{:S(2)}) copy-start(f32[32,512]{1,0:T(8,128)} %copy-done.38) | copy-start | bytes 196612
  234.3 13.8 %copy-start.15 = (bf16[256,256]{0,1:T(8,128)(2,1)S(1)}, bf16[256,256]{0,1:T(8,128)(2,1)}, u32[]{:S(2)}) copy-start(bf16[256,256]{0,1:T(8,128)(2,1)} %copy-done.14) | copy-start | bytes 393220
  234.3 14.9 %copy-start.66 = (bf16[256,128]{1,0:T(8,128)(2,1)S(1)}, bf16[256,128]{1,0:T(8,128)(2,1)}, u32[]{:S(2)}) copy-start(bf16[256,128]{1,0:T(8,128)(2,1)} %fusion.61) | copy-start | bytes 196612
  244.7 5.2 %collective-permute-start.8 = (bf16[248,512]{1,0:T(8,128)(2,1)}, bf16[248,512]{1,0:T(8,128)(2,1)S(1)}, u32[]{:S(2)}, u32[]{:S(2)}) collective-permute-start(bf16[248,512]{1,0:T(8,128)(2,1)} %constant_dynamic-update-slice_fusion.4), channel_id=1, source_target_pairs={{0,16},{16,0},{32,48},{48,32},{64,80},{80,64},{96,112},{112,96},{1... | collective-permute-start | bytes 761864 | tf_op jit(solution)/shard_map/ppermute | solution.py:52
  (94 other events, 267.5 us)
Sparse Core Ops, SparseCore 0:
  13.6 73.3 all-gather.1
where the time goes:
time: 261 us; the launch traced here: 260 us
  waiting for transfers between devices  65.4 us (25%)
  matrix products  55.1 us (21%)
  starting transfers between devices  41.8 us (16%)
  local copies, waits for them, and re-layouts  30.9 us (12%)
  blocking collectives  25.6 us (10%)
  other arithmetic  24.1 us (9%)
  between operations  16.8 us (6%)
    all_gather x1, waiting for transfers between devices, body(): lax.all_gather(packed, 'ctx', axis=0, tiled=True)  56.8 us
    psum x1, blocking collectives, body(): squares = lax.psum(jnp.sum(scaled * scaled, axis=1), 'head')  25.6 us
    ppermute x5, starting transfers between devices, from_partner(): return lax.ppermute(value, axis, pairs)  20.5 us
    dot_general x10, matrix products, body(): jnp.dot(ds_far, coarse_k[level_idx], preferred_element_type=jnp.float32)  12.6 us
    dot_general x10, matrix products, body(): jnp.dot(weights_bf, coarse_v[level_idx], preferred_element_type=jnp.float32)  11.6 us
    ppermute x2, starting transfers between devices, passed_along(): return lax.ppermute(value, axis, pairs)  11.2 us
    dot_general x10, matrix products, body(): jnp.einsum('tk,td->kd', weight_far[level_idx], d_out, preferred_element_t...  9.72 us
    ppermute x5, waiting for transfers between devices, from_partner(): return lax.ppermute(value, axis, pairs)  8.53 us
  transfers between devices with their start and end apart: 10, of which 3 were waited for; matrix products, arithmetic and copies ran while one was open for 17% of the time, Pallas kernels for 0%

commit v1 on v0

--- a/solution.py
+++ b/solution.py
@@ -106,9 +106,9 @@
     group_pair = list(pooled)
     shared = [level_idx for level_idx in range(LEV) if groups[level_idx] > 1]
     packed = jnp.concatenate([pooled[level_idx] for level_idx in shared], axis=0)
-    everyone = lax.all_gather(packed, "ctx", axis=0, tiled=True).reshape(
-        ctx_count, packed.shape[0], columns
-    )
+    everyone = jnp.concatenate(
+        lax.all_to_all(jnp.stack([packed] * lax.axis_size("ctx")), "ctx", 0, 0), axis=0
+    ).reshape(ctx_count, packed.shape[0], columns)
     offset = 0
     for level_idx in shared:
         count_rows = pooled[level_idx].shape[0]

time: 261 us -> 296 us (1.13)
  waiting for transfers between devices: 65.4 us -> 102 us
  between operations: 16.8 us -> 3.38 us
  starting transfers between devices: 41.8 us -> 47.9 us
  local copies, waits for them, and re-layouts: 30.9 us -> 34.2 us
    ppermute x1, waiting for transfers between devices: 0.01 us -> 86.1 us  [padded_2(): lax.ppermute(tail, axis, [(i, (i + 1) % count) for i in range(ends)])]
    all_gather x1 -> x0, waiting for transfers between devices: 56.8 us -> none  [body(): lax.all_gather(packed, 'ctx', axis=0, tiled=True)]
    all_to_all x0 -> x1, starting transfers between devices: none -> 11.6 us  [body(): lax.all_to_all(jnp.stack([packed] * lax.axis_size('ctx')), 'ctx', 0, 0)]
    ppermute x1, waiting for transfers between devices: 0.01 us -> 4.7 us  [padded_2(): lax.ppermute(head, axis, [((i + 1) % count, i) for i in range(ends)])]
    another operation x0 -> x1, local copies, waits for them, and re-layouts: none -> 3.74 us  [body(): jnp.stack([packed] * lax.axis_size('ctx'))]
    ppermute x1, starting transfers between devices: 5.57 us -> 2.1 us  [padded_2(): lax.ppermute(head, axis, [((i + 1) % count, i) for i in range(ends)])]
  transfers between devices with their start and end apart: 10 -> 10, of which waited for: 3 -> 4; matrix products, arithmetic and copies ran while one was open for 17% -> 15% of each run, Pallas kernels for 0% -> 0%
where the time goes in v1:
time: 296 us; the launch traced here: 294 us
  waiting for transfers between devices  102 us (34%)
  matrix products  55.1 us (19%)
  starting transfers between devices  47.9 us (16%)
  local copies, waits for them, and re-layouts  34.2 us (12%)
  blocking collectives  27.4 us (9%)
  other arithmetic  24.5 us (8%)
  between operations  3.38 us (1%)
    ppermute x1, waiting for transfers between devices, padded_2(): lax.ppermute(tail, axis, [(i, (i + 1) % count) for i in range(ends)])  86.1 us
    psum x1, blocking collectives, body(): squares = lax.psum(jnp.sum(scaled * scaled, axis=1), 'head')  27.4 us
    ppermute x5, starting transfers between devices, from_partner(): return lax.ppermute(value, axis, pairs)  19.6 us
    dot_general x10, matrix products, body(): jnp.dot(ds_far, coarse_k[level_idx], preferred_element_type=jnp.float32)  12.6 us
    dot_general x10, matrix products, body(): jnp.dot(weights_bf, coarse_v[level_idx], preferred_element_type=jnp.float32)  11.6 us
    all_to_all x1, starting transfers between devices, body(): lax.all_to_all(jnp.stack([packed] * lax.axis_size('ctx')), 'ctx', 0, 0)  11.6 us
    ppermute x2, starting transfers between devices, passed_along(): return lax.ppermute(value, axis, pairs)  11 us
    ppermute x5, waiting for transfers between devices, from_partner(): return lax.ppermute(value, axis, pairs)  10.9 us
  transfers between devices with their start and end apart: 10, of which 4 were waited for; matrix products, arithmetic and copies ran while one was open for 15% of the time, Pallas kernels for 0%

profile of v1, /device:TPU:1, one launch (start us, length us, event | category | flops | bytes accessed | tf_op | source)
XLA Modules:
  0.0 294.2 jit_solution(39906001335484462)
XLA Ops:
  0.7 1.0 concatenate.87
  1.7 0.9 concatenate.90
  2.6 1.0 concatenate.88
  3.6 0.9 concatenate.91
  6.1 3.7 %stack.2 = bf16[32,248,512]{2,1,0:T(8,128)(2,1)} broadcast(bf16[248,512]{1,0:T(8,128)(2,1)S(1)} %constant_dynamic-update-slice_fusion.2), dimensions={1,2} | broadcast | bytes 8380416 | tf_op jit(solution)/shard_map/stack | solution.py:110
  9.8 11.6 %all-to-all-start = ((bf16[32,248,512]{2,1,0:T(8,128)(2,1)}), bf16[32,248,512]{2,1,0:T(8,128)(2,1)}, u32[]{:S(2)}, u32[]{:S(2)}) async-start(bf16[32,248,512]{2,1,0:T(8,128)(2,1)} %stack.2), calls=%async_computation | async-start | bytes 16252928 | tf_op jit(solution)/shard_map/all_to_all | solution.py:110
  21.4 3.5 %collective-permute-start = (bf16[256,512]{1,0:T(8,128)(2,1)S(1)}, bf16[256,512]{1,0:T(8,128)(2,1)S(1)}, u32[]{:S(2)}, u32[]{:S(2)}) collective-permute-start(bf16[256,512]{1,0:T(8,128)(2,1)S(1)} %constant_dynamic-update-slice_fusion), channel_id=1, source_target_pairs={{0,16},{16,32},{32,48},{48,64},{64,80},{80,96},{96,112},{112,128},... | collective-permute-start | bytes 786440 | tf_op jit(solution)/shard_map/ppermute | solution.py:26
  25.0 2.1 collective-permute-start.1
  29.7 86.1 %collective-permute-done = bf16[256,512]{1,0:T(8,128)(2,1)S(1)} collective-permute-done((bf16[256,512]{1,0:T(8,128)(2,1)S(1)}, bf16[256,512]{1,0:T(8,128)(2,1)S(1)}, u32[]{:S(2)}, u32[]{:S(2)}) %collective-permute-start) | collective-permute-done | bytes 262176 | tf_op jit(solution)/shard_map/ppermute | solution.py:26
  115.8 4.7 %collective-permute-done.1 = bf16[256,512]{1,0:T(8,128)(2,1)S(1)} collective-permute-done((bf16[256,512]{1,0:T(8,128)(2,1)S(1)}, bf16[256,512]{1,0:T(8,128)(2,1)S(1)}, u32[]{:S(2)}, u32[]{:S(2)}) %collective-permute-start.1) | collective-permute-done | bytes 262176 | tf_op jit(solution)/shard_map/ppermute | solution.py:28
  122.3 1.1 fusion.272
  124.0 2.6 slice.349
  127.2 1.9 slice.351
  129.7 1.4 slice.353
  131.7 1.2 slice.355
  133.6 1.0 slice_bitcast_fusion
  139.7 1.1 fusion.101
  140.8 1.7 copy.106
  142.5 1.3 convolution_add_fusion.19
  143.8 1.3 convolution_add_fusion.18
  145.1 1.0 convolution_add_fusion.17
  146.2 1.0 convolution_add_fusion.16
  147.2 1.1 fusion.97
  148.3 1.7 copy.225
  150.0 1.2 convolution_add_fusion.14
  151.3 1.3 convolution_add_fusion.13
  152.6 1.0 convolution_add_fusion.12
  154.1 1.5 broadcast_multiply_fusion.1
  155.6 1.7 broadcast_multiply_fusion
  158.0 27.4 %all-reduce = (f32[256]{0:T(256)}, f32[256]{0:T(256)}) all-reduce(f32[256]{0:T(256)} %get-tuple-element.17, f32[256]{0:T(256)} %get-tuple-element.16), channel_id=1, replica_groups=mesh['ctx'=32,'head'=16] {'head'}, use_global_device_ids=true, to_apply=%region_30.31 | all-reduce | flops 512 | bytes 4096 | tf_op jit(solution)/shard_map/psum | solution.py:197
  186.2 1.8 subtract_multiply_fusion
  187.9 2.2 multiply_reduce_fusion.3
  190.2 1.9 fusion.130
  192.2 1.7 fusion.127
  193.9 0.9 fusion.115
  205.5 0.9 fusion.289
  206.9 0.9 fusion.290
  212.2 4.6 %collective-permute-start.4 = (bf16[128,512]{1,0:T(8,128)(2,1)}, bf16[128,512]{1,0:T(8,128)(2,1)}, u32[]{:S(2)}, u32[]{:S(2)}) collective-permute-start(bf16[128,512]{1,0:T(8,128)(2,1)} %select_convert_fusion), channel_id=1, source_target_pairs={{0,256},{16,272},{32,288},{48,304},{64,320},{80,336},{96,352},{112... | collective-permute-start | bytes 393224 | tf_op jit(solution)/shard_map/ppermute | solution.py:52
  220.3 1.7 reshape.808
  222.0 2.8 fusion.288
  226.0 8.6 %collective-permute-start.2 = (bf16[256,512]{1,0:T(8,128)(2,1)}, bf16[256,512]{1,0:T(8,128)(2,1)}, u32[]{:S(2)}, u32[]{:S(2)}) collective-permute-start(bf16[256,512]{1,0:T(8,128)(2,1)} %convert_element_type.240), channel_id=1, source_target_pairs={{16,0},{32,16},{48,32},{64,48},{80,64},{96,80},{112,96},{128,112},... | collective-permute-start | bytes 786440 | tf_op jit(solution)/shard_map/ppermute | solution.py:38
  235.6 2.4 collective-permute-start.3
  238.0 1.1 convolution_add_fusion.9
  239.2 1.2 convolution_add_fusion.8
  240.4 1.1 convolution_add_fusion.7
  241.6 1.1 convolution_add_fusion.6
  242.7 1.2 convolution_add_fusion.4
  243.9 1.1 convolution_add_fusion.3
  245.1 1.8 convolution_add_fusion.2
  247.3 1.1 convert_add_fusion.3
  248.4 1.9 collective-permute-start.5
  250.4 5.5 %collective-permute-done.5 = bf16[192,512]{1,0:T(8,128)(2,1)S(1)} collective-permute-done((bf16[192,512]{1,0:T(8,128)(2,1)S(1)}, bf16[192,512]{1,0:T(8,128)(2,1)S(1)}, u32[]{:S(2)}, u32[]{:S(2)}) %collective-permute-start.5) | collective-permute-done | bytes 196640 | tf_op jit(solution)/shard_map/ppermute | solution.py:52
  256.0 7.1 %collective-permute-start.6 = (bf16[224,512]{1,0:T(8,128)(2,1)S(1)}, bf16[224,512]{1,0:T(8,128)(2,1)S(1)}, u32[]{:S(2)}, u32[]{:S(2)}) collective-permute-start(bf16[224,512]{1,0:T(8,128)(2,1)S(1)} %pad_maximum_fusion.9), channel_id=1, source_target_pairs={{0,64},{16,80},{32,96},{48,112},{64,0},{80,16},{96,32},{112,48},{1... | collective-permute-start | bytes 688136 | tf_op jit(solution)/shard_map/ppermute | solution.py:52
  263.8 5.4 %collective-permute-done.6 = bf16[224,512]{1,0:T(8,128)(2,1)S(1)} collective-permute-done((bf16[224,512]{1,0:T(8,128)(2,1)S(1)}, bf16[224,512]{1,0:T(8,128)(2,1)S(1)}, u32[]{:S(2)}, u32[]{:S(2)}) %collective-permute-start.6) | collective-permute-done | bytes 229408 | tf_op jit(solution)/shard_map/ppermute | solution.py:52
  270.2 2.2 collective-permute-start.7
  272.4 1.7 fusion.61
  274.1 1.1 slice.379
  275.2 1.5 slice.299
  276.7 1.7 copy.168
  278.4 1.2 convolution_add_fusion.1
  279.7 1.0 convert_add_fusion
  285.6 3.8 %collective-permute-start.8 = (bf16[248,512]{1,0:T(8,128)(2,1)}, bf16[248,512]{1,0:T(8,128)(2,1)S(1)}, u32[]{:S(2)}, u32[]{:S(2)}) collective-permute-start(bf16[248,512]{1,0:T(8,128)(2,1)} %constant_dynamic-update-slice_fusion.4), channel_id=1, source_target_pairs={{0,16},{16,0},{32,48},{48,32},{64,80},{80,64},{96,112},{112,96},{1... | collective-permute-start | bytes 761864 | tf_op jit(solution)/shard_map/ppermute | solution.py:52
  289.4 1.1 fusion.60
  292.2 1.3 fusion.62
  (440 shorter events, 45.0 us)
Async XLA Ops:
  9.8 18.6 %copy-start.132 = (f32[2]{0:T(128)S(1)}, f32[2]{0:T(128)}, u32[]{:S(2)}) copy-start(f32[2]{0:T(128)} %param.13) | copy-start | bytes 28
  9.8 19.3 %copy-start.145 = (s32[2]{0:T(128)S(1)}, s32[2]{0:T(128)}, u32[]{:S(2)}) copy-start(s32[2]{0:T(128)} %param.12) | copy-start | bytes 28
  9.8 19.5 %copy-start.144 = (s32[2,4]{1,0:T(2,128)S(1)}, s32[2,4]{1,0:T(2,128)}, u32[]{:S(2)}) copy-start(s32[2,4]{1,0:T(2,128)} %param.11) | copy-start | bytes 100
  9.8 19.7 %copy-start.70 = (bf16[256,256]{1,0:T(8,128)(2,1)S(1)}, bf16[256,256]{1,0:T(8,128)(2,1)}, u32[]{:S(2)}) copy-start(bf16[256,256]{1,0:T(8,128)(2,1)} %param.15) | copy-start | bytes 393220
  9.8 19.9 %copy-start = (bf16[256,256]{1,0:T(8,128)(2,1)S(1)}, bf16[256,256]{1,0:T(8,128)(2,1)}, u32[]{:S(2)}) copy-start(bf16[256,256]{1,0:T(8,128)(2,1)} %param.8) | copy-start | bytes 393220
  9.8 114.2 %all-to-all-start = ((bf16[32,248,512]{2,1,0:T(8,128)(2,1)}), bf16[32,248,512]{2,1,0:T(8,128)(2,1)}, u32[]{:S(2)}, u32[]{:S(2)}) async-start(bf16[32,248,512]{2,1,0:T(8,128)(2,1)} %stack.2), calls=%async_computation | async-start | bytes 16252928 | tf_op jit(solution)/shard_map/all_to_all | solution.py:110
  21.4 94.4 %collective-permute-start = (bf16[256,512]{1,0:T(8,128)(2,1)S(1)}, bf16[256,512]{1,0:T(8,128)(2,1)S(1)}, u32[]{:S(2)}, u32[]{:S(2)}) collective-permute-start(bf16[256,512]{1,0:T(8,128)(2,1)S(1)} %constant_dynamic-update-slice_fusion), channel_id=1, source_target_pairs={{0,16},{16,32},{32,48},{48,64},{64,80},{80,96},{96,112},{112,128},... | collective-permute-start | bytes 786440 | tf_op jit(solution)/shard_map/ppermute | solution.py:26
  25.0 95.6 %collective-permute-start.1 = (bf16[256,512]{1,0:T(8,128)(2,1)S(1)}, bf16[256,512]{1,0:T(8,128)(2,1)S(1)}, u32[]{:S(2)}, u32[]{:S(2)}) collective-permute-start(bf16[256,512]{1,0:T(8,128)(2,1)S(1)} %constant_dynamic-update-slice_fusion), channel_id=1, source_target_pairs={{16,0},{32,16},{48,32},{64,48},{80,64},{96,80},{112,96},{128,112},... | collective-permute-start | bytes 786440 | tf_op jit(solution)/shard_map/ppermute | solution.py:28
  27.1 102.2 %copy-start.82 = (s32[256]{0:T(256)}, s32[256]{0:T(256)S(1)}, u32[]{:S(2)}) copy-start(s32[256]{0:T(256)S(1)} %get-tuple-element.97) | copy-start | bytes 3076
  27.2 104.2 %copy-start.97 = (s32[256]{0:T(256)}, s32[256]{0:T(256)S(1)}, u32[]{:S(2)}) copy-start(s32[256]{0:T(256)S(1)} %get-tuple-element.96) | copy-start | bytes 3076
  27.2 104.2 %copy-start.100 = (s32[256]{0:T(256)}, s32[256]{0:T(256)S(1)}, u32[]{:S(2)}) copy-start(s32[256]{0:T(256)S(1)} %get-tuple-element.94) | copy-start | bytes 3076
  27.2 104.2 %copy-start.103 = (s32[256]{0:T(256)}, s32[256]{0:T(256)S(1)}, u32[]{:S(2)}) copy-start(s32[256]{0:T(256)S(1)} %get-tuple-element.95) | copy-start | bytes 3076
  27.8 105.4 %copy-start.106 = (s32[256]{0:T(256)}, s32[256]{0:T(256)S(1)}, u32[]{:S(2)}) copy-start(s32[256]{0:T(256)S(1)} %get-tuple-element.91) | copy-start | bytes 3076
  28.4 98.5 %copy-start.85 = (s32[256]{0:T(256)}, s32[256]{0:T(256)S(1)}, u32[]{:S(2)}) copy-start(s32[256]{0:T(256)S(1)} %get-tuple-element.101) | copy-start | bytes 3076
  28.5 100.9 %copy-start.111 = (s32[256]{0:T(256)}, s32[256]{0:T(256)S(1)}, u32[]{:S(2)}) copy-start(s32[256]{0:T(256)S(1)} %get-tuple-element.98) | copy-start | bytes 3076
  28.5 100.9 %copy-start.114 = (s32[256]{0:T(256)}, s32[256]{0:T(256)S(1)}, u32[]{:S(2)}) copy-start(s32[256]{0:T(256)S(1)} %get-tuple-element.99) | copy-start | bytes 3076
  29.3 103.9 %copy-start.117 = (s32[256]{0:T(256)}, s32[256]{0:T(256)S(1)}, u32[]{:S(2)}) copy-start(s32[256]{0:T(256)S(1)} %get-tuple-element.92) | copy-start | bytes 3076
  29.3 103.9 %copy-start.122 = (s32[256]{0:T(256)}, s32[256]{0:T(256)S(1)}, u32[]{:S(2)}) copy-start(s32[256]{0:T(256)S(1)} %get-tuple-element.93) | copy-start | bytes 3076
  29.5 92.5 %copy-start.133 = (s32[8]{0:T(128)}, s32[8]{0:T(128)S(1)}, u32[]{:S(2)}) copy-start(s32[8]{0:T(128)S(1)} %eq.37) | copy-start | bytes 100
  123.7 11.4 %copy-start.80 = (f32[2,128]{1,0:T(2,128)}, f32[2,128]{1,0:T(2,128)S(1)}, u32[]{:S(2)}) copy-start(f32[2,128]{1,0:T(2,128)S(1)} %get-tuple-element.80) | copy-start | bytes 3076
  124.0 12.0 %copy-start.79 = (f32[2,128]{1,0:T(2,128)}, f32[2,128]{1,0:T(2,128)S(1)}, u32[]{:S(2)}) copy-start(f32[2,128]{1,0:T(2,128)S(1)} %get-tuple-element.68) | copy-start | bytes 3076
  126.7 76.9 %copy-start.7 = (bf16[2,128,512]{2,1,0:T(8,128)(2,1)}, bf16[2,128,512]{2,1,0:T(8,128)(2,1)S(1)}, u32[]{:S(2)}) copy-start(bf16[2,128,512]{2,1,0:T(8,128)(2,1)S(1)} %constant_dynamic-slice_fusion.3) | copy-start | bytes 786436
  126.9 23.0 %copy-start.39 = (f32[256,256]{0,1:T(8,128)}, f32[256,256]{0,1:T(8,128)S(1)}, u32[]{:S(2)}) copy-start(f32[256,256]{0,1:T(8,128)S(1)} %get-tuple-element.79) | copy-start | bytes 786436
  127.2 9.7 %copy-start.41 = (f32[256,256]{0,1:T(8,128)}, f32[256,256]{0,1:T(8,128)S(1)}, u32[]{:S(2)}) copy-start(f32[256,256]{0,1:T(8,128)S(1)} %get-tuple-element.67) | copy-start | bytes 786436
  129.1 71.7 %copy-start.8 = (bf16[4,64,512]{2,1,0:T(8,128)(2,1)}, bf16[4,64,512]{2,1,0:T(8,128)(2,1)S(1)}, u32[]{:S(2)}) copy-start(bf16[4,64,512]{2,1,0:T(8,128)(2,1)S(1)} %constant_dynamic-slice_fusion.2) | copy-start | bytes 786436
  129.4 7.9 %copy-start.43 = (f32[256,256]{0,1:T(8,128)}, f32[256,256]{0,1:T(8,128)S(1)}, u32[]{:S(2)}) copy-start(f32[256,256]{0,1:T(8,128)S(1)} %get-tuple-element.77) | copy-start | bytes 786436
  131.1 65.1 %copy-start.9 = (bf16[8,32,512]{2,1,0:T(8,128)(2,1)}, bf16[8,32,512]{2,1,0:T(8,128)(2,1)S(1)}, u32[]{:S(2)}) copy-start(bf16[8,32,512]{2,1,0:T(8,128)(2,1)S(1)} %constant_dynamic-slice_fusion.1) | copy-start | bytes 786436
  132.9 108.6 %copy-start.6 = (bf16[16,16,512]{2,1,0:T(8,128)(2,1)}, bf16[16,16,512]{2,1,0:T(8,128)(2,1)S(1)}, u32[]{:S(2)}) copy-start(bf16[16,16,512]{2,1,0:T(8,128)(2,1)S(1)} %constant_dynamic-slice_fusion) | copy-start | bytes 786436
  134.6 63.4 %copy-start.10 = (bf16[256,512]{1,0:T(8,128)(2,1)}, bf16[256,512]{1,0:T(8,128)(2,1)S(1)}, u32[]{:S(2)}) copy-start(bf16[256,512]{1,0:T(8,128)(2,1)S(1)} %slice_bitcast_fusion) | copy-start | bytes 786436
  155.6 30.5 %copy-start.27 = (f32[256,128]{0,1:T(8,128)}, f32[256,128]{0,1:T(8,128)S(1)}, u32[]{:S(2)}) copy-start(f32[256,128]{0,1:T(8,128)S(1)} %get-tuple-element.84) | copy-start | bytes 393220
  157.3 28.8 %copy-start.28 = (f32[256,128]{0,1:T(8,128)}, f32[256,128]{0,1:T(8,128)S(1)}, u32[]{:S(2)}) copy-start(f32[256,128]{0,1:T(8,128)S(1)} %get-tuple-element.82) | copy-start | bytes 393220
  196.0 11.8 %copy-start.21 = (bf16[256,256]{0,1:T(8,128)(2,1)}, bf16[256,256]{0,1:T(8,128)(2,1)S(1)}, u32[]{:S(2)}) copy-start(bf16[256,256]{0,1:T(8,128)(2,1)S(1)} %fusion.50) | copy-start | bytes 393220
  196.2 13.3 %copy-start.20 = (bf16[256,256]{0,1:T(8,128)(2,1)}, bf16[256,256]{0,1:T(8,128)(2,1)S(1)}, u32[]{:S(2)}) copy-start(bf16[256,256]{0,1:T(8,128)(2,1)S(1)} %fusion.51) | copy-start | bytes 393220
  196.5 12.2 %copy-start.18 = (bf16[256,256]{0,1:T(8,128)(2,1)}, bf16[256,256]{0,1:T(8,128)(2,1)S(1)}, u32[]{:S(2)}) copy-start(bf16[256,256]{0,1:T(8,128)(2,1)S(1)} %fusion.55) | copy-start | bytes 393220
  197.2 13.1 %copy-start.15 = (bf16[256,256]{0,1:T(8,128)(2,1)}, bf16[256,256]{0,1:T(8,128)(2,1)S(1)}, u32[]{:S(2)}) copy-start(bf16[256,256]{0,1:T(8,128)(2,1)S(1)} %fusion.56) | copy-start | bytes 393220
  198.0 13.1 %copy-start.16 = (bf16[256,256]{0,1:T(8,128)(2,1)}, bf16[256,256]{0,1:T(8,128)(2,1)S(1)}, u32[]{:S(2)}) copy-start(bf16[256,256]{0,1:T(8,128)(2,1)S(1)} %fusion.52) | copy-start | bytes 393220
  198.7 12.6 %copy-start.13 = (bf16[256,256]{0,1:T(8,128)(2,1)}, bf16[256,256]{0,1:T(8,128)(2,1)S(1)}, u32[]{:S(2)}) copy-start(bf16[256,256]{0,1:T(8,128)(2,1)S(1)} %fusion.57) | copy-start | bytes 393220
  200.8 16.0 %copy-start.24 = (bf16[256,256]{0,1:T(8,128)(2,1)}, bf16[256,256]{0,1:T(8,128)(2,1)S(1)}, u32[]{:S(2)}) copy-start(bf16[256,256]{0,1:T(8,128)(2,1)S(1)} %fusion.49) | copy-start | bytes 393220
  201.5 16.1 %copy-start.22 = (bf16[256,256]{0,1:T(8,128)(2,1)}, bf16[256,256]{0,1:T(8,128)(2,1)S(1)}, u32[]{:S(2)}) copy-start(bf16[256,256]{0,1:T(8,128)(2,1)S(1)} %fusion.54) | copy-start | bytes 393220
  203.5 14.9 %copy-start.26 = (bf16[256,256]{0,1:T(8,128)(2,1)}, bf16[256,256]{0,1:T(8,128)(2,1)S(1)}, u32[]{:S(2)}) copy-start(bf16[256,256]{0,1:T(8,128)(2,1)S(1)} %fusion.48) | copy-start | bytes 393220
  203.8 15.5 %copy-start.25 = (bf16[256,256]{0,1:T(8,128)(2,1)}, bf16[256,256]{0,1:T(8,128)(2,1)S(1)}, u32[]{:S(2)}) copy-start(bf16[256,256]{0,1:T(8,128)(2,1)S(1)} %fusion.53) | copy-start | bytes 393220
  212.2 35.1 %collective-permute-start.4 = (bf16[128,512]{1,0:T(8,128)(2,1)}, bf16[128,512]{1,0:T(8,128)(2,1)}, u32[]{:S(2)}, u32[]{:S(2)}) collective-permute-start(bf16[128,512]{1,0:T(8,128)(2,1)} %select_convert_fusion), channel_id=1, source_target_pairs={{0,256},{16,272},{32,288},{48,304},{64,320},{80,336},{96,352},{112... | collective-permute-start | bytes 393224 | tf_op jit(solution)/shard_map/ppermute | solution.py:52
  224.7 13.3 %copy-start.11 = (f32[2,128,128]{2,1,0:T(8,128)S(1)}, f32[2,128,128]{2,1,0:T(8,128)}, u32[]{:S(2)}) copy-start(f32[2,128,128]{2,1,0:T(8,128)} %fusion.289) | copy-start | bytes 393220
  226.0 16.7 %copy-start.12 = (f32[2,128,128]{2,1,0:T(8,128)S(1)}, f32[2,128,128]{2,1,0:T(8,128)}, u32[]{:S(2)}) copy-start(f32[2,128,128]{2,1,0:T(8,128)} %fusion.290) | copy-start | bytes 393220
  226.0 66.1 %collective-permute-start.2 = (bf16[256,512]{1,0:T(8,128)(2,1)}, bf16[256,512]{1,0:T(8,128)(2,1)}, u32[]{:S(2)}, u32[]{:S(2)}) collective-permute-start(bf16[256,512]{1,0:T(8,128)(2,1)} %convert_element_type.240), channel_id=1, source_target_pairs={{16,0},{32,16},{48,32},{64,48},{80,64},{96,80},{112,96},{128,112},... | collective-permute-start | bytes 786440 | tf_op jit(solution)/shard_map/ppermute | solution.py:38
  235.6 8.3 %copy-start.23 = (bf16[256,256]{0,1:T(8,128)(2,1)S(1)}, bf16[256,256]{0,1:T(8,128)(2,1)}, u32[]{:S(2)}) copy-start(bf16[256,256]{0,1:T(8,128)(2,1)} %copy-done.22) | copy-start | bytes 393220
  235.6 9.4 %copy-start.19 = (bf16[256,256]{0,1:T(8,128)(2,1)S(1)}, bf16[256,256]{0,1:T(8,128)(2,1)}, u32[]{:S(2)}) copy-start(bf16[256,256]{0,1:T(8,128)(2,1)} %copy-done.18) | copy-start | bytes 393220
  235.6 11.3 %copy-start.31 = (f32[256,128]{1,0:T(8,128)S(1)}, f32[256,128]{1,0:T(8,128)}, u32[]{:S(2)}) copy-start(f32[256,128]{1,0:T(8,128)} %convolution_multiply_fusion.19) | copy-start | bytes 393220
  235.6 11.3 %copy-start.32 = (f32[256,128]{1,0:T(8,128)S(1)}, f32[256,128]{1,0:T(8,128)}, u32[]{:S(2)}) copy-start(f32[256,128]{1,0:T(8,128)} %convolution_multiply_fusion.18) | copy-start | bytes 393220
  235.6 11.3 %copy-start.73 = (f32[256,128]{1,0:T(8,128)S(1)}, f32[256,128]{1,0:T(8,128)}, u32[]{:S(2)}) copy-start(f32[256,128]{1,0:T(8,128)} %fusion.130) | copy-start | bytes 393220
  235.6 11.2 %copy-start.74 = (f32[256,128]{1,0:T(8,128)S(1)}, f32[256,128]{1,0:T(8,128)}, u32[]{:S(2)}) copy-start(f32[256,128]{1,0:T(8,128)} %fusion.115) | copy-start | bytes 393220
  235.6 56.5 %collective-permute-start.3 = (bf16[256,512]{1,0:T(8,128)(2,1)}, bf16[256,512]{1,0:T(8,128)(2,1)}, u32[]{:S(2)}, u32[]{:S(2)}) collective-permute-start(bf16[256,512]{1,0:T(8,128)(2,1)} %convert_element_type.242), channel_id=1, source_target_pairs={{0,16},{16,32},{32,48},{48,64},{64,80},{80,96},{96,112},{112,128},... | collective-permute-start | bytes 786440 | tf_op jit(solution)/shard_map/ppermute | solution.py:38
  239.2 7.8 %copy-start.29 = (f32[256,128]{1,0:T(8,128)S(1)}, f32[256,128]{1,0:T(8,128)}, u32[]{:S(2)}) copy-start(f32[256,128]{1,0:T(8,128)} %convolution_multiply_fusion.17) | copy-start | bytes 393220
  247.2 8.8 %copy-start.3 = (f32[256,512]{1,0:T(8,128)}, f32[256,512]{1,0:T(8,128)S(1)}, u32[]{:S(2)}) copy-start(f32[256,512]{1,0:T(8,128)S(1)} %pad_maximum_fusion.3) | copy-start | bytes 1572868
  248.4 7.5 %collective-permute-start.5 = (bf16[192,512]{1,0:T(8,128)(2,1)S(1)}, bf16[192,512]{1,0:T(8,128)(2,1)S(1)}, u32[]{:S(2)}, u32[]{:S(2)}) collective-permute-start(bf16[192,512]{1,0:T(8,128)(2,1)S(1)} %pad_maximum_fusion.10), channel_id=1, source_target_pairs={{0,128},{16,144},{32,160},{48,176},{64,192},{80,208},{96,224},{112... | collective-permute-start | bytes 589832 | tf_op jit(solution)/shard_map/ppermute | solution.py:52
  255.9 16.5 %copy-start.17 = (bf16[256,256]{0,1:T(8,128)(2,1)S(1)}, bf16[256,256]{0,1:T(8,128)(2,1)}, u32[]{:S(2)}) copy-start(bf16[256,256]{0,1:T(8,128)(2,1)} %copy-done.16) | copy-start | bytes 393220
  256.0 13.2 %collective-permute-start.6 = (bf16[224,512]{1,0:T(8,128)(2,1)S(1)}, bf16[224,512]{1,0:T(8,128)(2,1)S(1)}, u32[]{:S(2)}, u32[]{:S(2)}) collective-permute-start(bf16[224,512]{1,0:T(8,128)(2,1)S(1)} %pad_maximum_fusion.9), channel_id=1, source_target_pairs={{0,64},{16,80},{32,96},{48,112},{64,0},{80,16},{96,32},{112,48},{1... | collective-permute-start | bytes 688136 | tf_op jit(solution)/shard_map/ppermute | solution.py:52
  269.4 11.2 %copy-start.5 = (f32[64,512]{1,0:T(8,128)}, f32[64,512]{1,0:T(8,128)S(1)}, u32[]{:S(2)}) copy-start(f32[64,512]{1,0:T(8,128)S(1)} %convert_add_fusion.5) | copy-start | bytes 393220
  269.4 10.3 %copy-start.4 = (f32[256,512]{1,0:T(8,128)S(1)}, f32[256,512]{1,0:T(8,128)}, u32[]{:S(2)}) copy-start(f32[256,512]{1,0:T(8,128)} %copy-done.3) | copy-start | bytes 1572868
  270.2 9.5 %collective-permute-start.7 = (bf16[240,512]{1,0:T(8,128)(2,1)}, bf16[240,512]{1,0:T(8,128)(2,1)}, u32[]{:S(2)}, u32[]{:S(2)}) collective-permute-start(bf16[240,512]{1,0:T(8,128)(2,1)} %pad_maximum_fusion.8), channel_id=1, source_target_pairs={{0,32},{16,48},{32,0},{48,16},{64,96},{80,112},{96,64},{112,80},{1... | collective-permute-start | bytes 737288 | tf_op jit(solution)/shard_map/ppermute | solution.py:52
  275.2 9.1 %copy-start.38 = (f32[32,512]{1,0:T(8,128)S(1)}, f32[32,512]{1,0:T(8,128)}, u32[]{:S(2)}) copy-start(f32[32,512]{1,0:T(8,128)} %copy-done.37) | copy-start | bytes 196612
  275.2 14.2 %copy-start.14 = (bf16[256,256]{0,1:T(8,128)(2,1)S(1)}, bf16[256,256]{0,1:T(8,128)(2,1)}, u32[]{:S(2)}) copy-start(bf16[256,256]{0,1:T(8,128)(2,1)} %copy-done.13) | copy-start | bytes 393220
  275.2 15.3 %copy-start.65 = (bf16[256,128]{1,0:T(8,128)(2,1)S(1)}, bf16[256,128]{1,0:T(8,128)(2,1)}, u32[]{:S(2)}) copy-start(bf16[256,128]{1,0:T(8,128)(2,1)} %fusion.61) | copy-start | bytes 196612
  285.6 5.6 %collective-permute-start.8 = (bf16[248,512]{1,0:T(8,128)(2,1)}, bf16[248,512]{1,0:T(8,128)(2,1)S(1)}, u32[]{:S(2)}, u32[]{:S(2)}) collective-permute-start(bf16[248,512]{1,0:T(8,128)(2,1)} %constant_dynamic-update-slice_fusion.4), channel_id=1, source_target_pairs={{0,16},{16,0},{32,48},{48,32},{64,80},{80,64},{96,112},{112,96},{1... | collective-permute-start | bytes 761864 | tf_op jit(solution)/shard_map/ppermute | solution.py:52
  (93 other events, 334.4 us)
